TPU v7x, 1024 devices: a whole 4x4x32 slice. The times are simulated.
1024 devices in a mesh: dp: 256 (over x, z, core), tensor: 4 (over y).
Axes of the slice: x: 4, y: 4, z: 32, core: 2. Of those that a mesh axis runs over, the one named last changes fastest.
Arguments:
- out_grad: bfloat16 [49152, 4096], P('dp'), may hold values from -24 to 24
- saved_input: bfloat16 [49152, 2048], P('dp', 'tensor'), may hold values from -6 to 6
- weight: bfloat16 [2048, 4096], P('tensor'), may hold values from -0.09375 to 0.09375
- amax_history: float32 [16], replicated, may hold values from 100 to 250
Outputs:
- input_grad: bfloat16 [49152, 2048], P('dp', 'tensor')
- weight_grad_q: bfloat16 [2048, 4096], P('tensor', 'dp')
- new_history: float32 [16], replicated
All inputs are finite; a program needn't handle non-finite values.
Results may differ from a plain program's by a relative error of at most 0.0051.
Values sent between devices are 32-bit elements; how exact they have to be, the bound alone decides.
A program may use at most 32 MiB of HBM per device.

v0:
```python
import jax
import jax.numpy as jnp
from jax import lax
from jax.sharding import PartitionSpec as P

LIMIT = 8.0


def quantize(term, scale_in):
    rounded = jnp.clip(term * scale_in, -LIMIT, LIMIT).astype(jnp.bfloat16)
    rounded = lax.optimization_barrier(rounded)
    return rounded.astype(jnp.float32)


def transposed_term(grads, inputs):
    return lax.dot_general(
        grads, inputs, (((0,), (0,)), ((), ())), preferred_element_type=jnp.float32
    )


def input_rows(grads, weight):
    return lax.dot_general(
        grads, weight, (((1,), (1,)), ((), ())), preferred_element_type=jnp.float32
    )


def shards(out_grad, saved_input, weight, amax_history):
    scale_in = LIMIT / jnp.max(amax_history)
    input_grad = input_rows(out_grad, weight).astype(jnp.bfloat16)
    summed = lax.psum_scatter(
        quantize(transposed_term(out_grad, saved_input), scale_in),
        "dp",
        scatter_dimension=0,
        tiled=True,
    )
    weight_sum = summed / scale_in
    local_peak = jnp.max(jnp.abs(weight_sum))
    amax = lax.pmax(local_peak, ("dp", "tensor"))
    new_history = jnp.concatenate([amax[None], amax_history[:-1]])
    out_scale = LIMIT / jnp.max(new_history)
    weight_grad_q = (weight_sum.T * out_scale).astype(jnp.bfloat16)
    return (input_grad, weight_grad_q, new_history)


def solution(mesh):
    placed = (P("dp", None), P("dp", "tensor"), P("tensor", None), P())
    return jax.shard_map(
        shards,
        mesh=mesh,
        in_specs=placed,
        out_specs=(P("dp", "tensor"), P("tensor", "dp"), P()),
        check_vma=False,
    )
```

profile of v0, /device:TPU:1, one launch (start us, length us, event | category | flops | bytes accessed | tf_op | source)
XLA Modules:
  0.0 703.6 jit_solution(10953286536992538091)
XLA Ops:
  7.2 0.0 copy-start
  7.2 0.0 reduce-scatter.2.cloned.1.call-start
  7.2 1.4 reduce_max.30
  9.3 0.0 copy-done
  9.3 2.2 clamp_convert_fusion
  11.6 4.4 convert_element_type.17
  16.0 0.0 reduce-scatter.2.cloned.1.call-update
  16.0 0.0 copy-start.1
  16.0 4.4 convolution_convert_fusion
  20.4 493.6 %reduce-scatter.2.cloned.1.call-done = f32[16,512]{1,0:T(8,128)} async-done(((f32[4096,512]{1,0:T(8,128)}), f32[16,512]{1,0:T(8,128)}) %reduce-scatter.2.cloned.1.call-update) | async-done | bytes 32784 | tf_op jit(solution)/shard_map/reduce_scatter | solution.py:30
  514.0 1.4 abs_reduce_fusion
  515.4 0.0 copy-done.1
  515.4 0.7 fusion.1
  516.1 176.7 %pmax.7 = f32[]{:T(128)} all-reduce(f32[]{:T(128)} %abs_reduce_fusion), channel_id=1, replica_groups=mesh['dp'=256,'tensor'=4] {'dp','tensor'}, use_global_device_ids=true, to_apply=%region_3.4 | all-reduce | flops 1 | bytes 8 | tf_op jit(solution)/shard_map/pmax | solution.py:38
  694.1 1.2 pad_maximum_fusion
  695.4 1.4 fusion
Async XLA Ops:
  7.2 2.1 copy-start
  7.2 506.9 %reduce-scatter.2.cloned.1.call-start = ((), (), s32[]{:S(2)}) async-start(), calls=%async_computation.1 | async-start | bytes 8421376 | tf_op jit(solution)/shard_map/reduce_scatter | solution.py:30
  16.0 499.4 %copy-start.1 = (f32[16]{0:T(128)S(1)}, f32[16]{0:T(128)}, u32[]{:S(2)}) copy-start(f32[16]{0:T(128)} %param.7) | copy-start | bytes 196
Sparse Core Ops, SparseCore 0:
  16.1 497.8 reduce-scatter.1
where the time goes:
time: 704 us
  waiting for transfers between devices  494 us (70%)
  blocking collectives  177 us (25%)
  between operations  16.1 us (2%)
  other arithmetic  10.4 us (1%)
    reduce_scatter x1, waiting for transfers between devices, shards(): lax.psum_scatter(quantize(transposed_term(out_grad, saved_input), scale_i...  494 us
    pmax x1, blocking collectives, shards(): amax = lax.pmax(local_peak, ('dp', 'tensor'))  177 us
  transfers between devices with their start and end apart: 1, of which 1 were waited for; matrix products, arithmetic and copies ran while one was open for 1% of the time, Pallas kernels for 0%

commit v1 on v0

v1 whole, which is shorter than its diff:
```python
import functools

import jax
import jax.numpy as jnp
from jax import lax
from jax.experimental import pallas as pl
from jax.experimental.pallas import tpu as pltpu
from jax.sharding import PartitionSpec as P

LIMIT = 8.0
MESH = pl.DeviceIdType.MESH
NX, NZ, NY = 4, 32, 4
NB = NZ // 4
F32 = jnp.float32


def kernel(
    og_hbm, si_hbm, w_hbm, hist_ref,
    ig_out, wq_out, hist_out,
    og, si, w, ig, terms, from_core, pass_one, in_one, pass_two, in_two,
    ready, in_last, peaks_core, peaks_plane, peaks_z, peaks_end, peak,
    local_sem, send_sem, recv_sem,
):
    dp, y = lax.axis_index("dp"), lax.axis_index("tensor")
    x, z, c = dp // (2 * NZ), lax.rem(dp // 2, NZ), lax.rem(dp, 2)
    zc = lax.rem(z, 4)

    def device(x, y, z, c):
        return ((x * NZ + z) * 2 + c, y)

    def along_x(d):
        return device(lax.rem(x + d + NX, NX), y, z, c)

    def along_z(d):
        return device(x, y, lax.rem(z + d + NZ, NZ), c)

    def in_plane(dx, dy):
        return device(lax.rem(x + dx, NX), lax.rem(y + dy, NY), z, c)

    other_core = device(x, y, z, 1 - c)

    barrier = pltpu.get_barrier_semaphore()

    def greet(to):
        pl.semaphore_signal(barrier, inc=1, device_id=to, device_id_type=MESH)

    @pl.loop(1, NZ)
    def _(d):
        greet(along_z(d))

    @pl.loop(1, NX * NY)
    def _(d):
        greet(in_plane(d // NY, lax.rem(d, NY)))

    greet(other_core)

    get_og = pltpu.make_async_copy(og_hbm, og, local_sem.at[0])
    get_si = pltpu.make_async_copy(si_hbm, si, local_sem.at[1])
    get_w = pltpu.make_async_copy(w_hbm, w, local_sem.at[2])
    get_si.start()
    get_og.start()
    get_w.start()

    used = [0]
    sent = []

    def send(src, dst, to):
        n = used[0]
        used[0] += 1
        copy = pltpu.make_async_remote_copy(
            src_ref=src, dst_ref=dst, send_sem=send_sem.at[n], recv_sem=recv_sem.at[n],
            device_id=to, device_id_type=MESH,
        )
        copy.start()
        sent.append(copy)
        return copy

    scale_in = LIMIT / jnp.max(hist_ref[...])
    get_si.wait()
    get_og.wait()

    def tile(at):
        @pl.loop(0, 4)
        def _(s):
            columns = pl.ds(pl.multiple_of(at * 1024 + s * 256, 256), 256)
            term = lax.dot_general(
                og[:, columns], si[...], (((0,), (0,)), ((), ())), preferred_element_type=F32
            )
            quant = jnp.clip(term * scale_in, -LIMIT, LIMIT).astype(jnp.bfloat16).astype(F32)
            for b in range(2):
                for j in range(4):
                    for core in range(2):
                        row = b * 128 + j * 32 + core * 16
                        terms[0, core, at, j, s * 2 + b] = quant[row : row + 8]
                        terms[1, core, j, at, s * 2 + b] = quant[row + 8 : row + 16]

    first, second = (x, zc), (zc, x)

    def classes(k):
        return [lax.rem(m + k, 4) for m in first]

    core_copies = [{}, {}]

    def to_core(p, k):
        m = classes(k)[p]
        core_copies[p][k] = send(terms.at[p, 1 - c, m], from_core.at[p, m], other_core)

    def add_core(p, k):
        core_copies[p][k].wait_recv()
        m = classes(k)[p]

        @pl.loop(0, 4)
        def _(i):
            terms[p, c, m, i] += from_core[p, m, i]

    order = (2, 1, 3, 0)
    for n, k in enumerate(order):
        tile(lax.rem(x + k, 4))
        if n == 0:
            pl.semaphore_wait(barrier, NZ - 1 + NX * NY - 1 + 1)
        to_core(0, k)
    for k in order:
        to_core(1, k)

    A, B = pl.ds(0, 2), pl.ds(2, 2)
    plus = (along_x(1), along_z(1))
    minus = (along_x(-1), along_z(-1))

    one = [{}, {}]
    for p in range(2):
        m = classes(2)[p]
        add_core(p, 2)
        one[p]["a+"] = send(terms.at[p, c, m, A], pass_one.at[p, 0], plus[p])
        one[p]["a-"] = send(terms.at[p, c, m, B], pass_one.at[p, 1], minus[p])
    for p in range(2):
        add_core(p, 1)
        one[p]["b+"] = send(terms.at[p, c, classes(1)[p], B], in_one.at[p, 0, B], plus[p])
        add_core(p, 3)
        one[p]["b-"] = send(terms.at[p, c, classes(3)[p], A], in_one.at[p, 1, A], minus[p])
    for p in range(2):
        m = classes(1)[p]
        one[p]["a+"].wait_recv()
        terms[p, c, m, A] += pass_one[p, 0]
        one[p]["c+"] = send(terms.at[p, c, m, A], in_one.at[p, 0, A], plus[p])
        m = classes(3)[p]
        one[p]["a-"].wait_recv()
        terms[p, c, m, B] += pass_one[p, 1]
        one[p]["c-"] = send(terms.at[p, c, m, B], in_one.at[p, 1, B], minus[p])
    for p in range(2):
        add_core(p, 0)

    get_w.wait()

    @pl.loop(0, 2)
    def _(i):
        rows = pl.ds(pl.multiple_of(i * 256, 256), 256)
        ig[:, rows] = lax.dot_general(
            og[...], w[rows, :], (((1,), (1,)), ((), ())), preferred_element_type=F32
        ).astype(jnp.bfloat16)

    put_ig = pltpu.make_async_copy(ig, ig_out, local_sem.at[3])
    put_ig.start()

    C, D = pl.ds(0, NB // 2), pl.ds(NB // 2, NB // 2)
    two = [{}, {}]
    up, down = (plus[1], plus[0]), (minus[1], minus[0])
    for p in range(2):
        for key in ("b+", "b-", "c+", "c-"):
            one[p][key].wait_recv()
        m, n = first[p], second[p]

        def total(k):
            q = lax.rem(n + k, 4)
            terms[p, c, m, q] += in_one[p, 0, q] + in_one[p, 1, q]
            return terms.at[p, c, m, q]

        unit = total(2)
        two[p]["a+"] = send(unit.at[C], pass_two.at[p, 0], up[p])
        two[p]["a-"] = send(unit.at[D], pass_two.at[p, 1], down[p])
        two[p]["b+"] = send(total(1).at[D], in_two.at[p, 0, D], up[p])
        two[p]["b-"] = send(total(3).at[C], in_two.at[p, 1, C], down[p])
        total(0)
    for p in range(2):
        m, n = first[p], second[p]
        q = lax.rem(n + 1, 4)
        two[p]["a+"].wait_recv()
        terms[p, c, m, q, C] += pass_two[p, 0]
        two[p]["c+"] = send(terms.at[p, c, m, q, C], in_two.at[p, 0, C], up[p])
        q = lax.rem(n + 3, 4)
        two[p]["a-"].wait_recv()
        terms[p, c, m, q, D] += pass_two[p, 1]
        two[p]["c-"] = send(terms.at[p, c, m, q, D], in_two.at[p, 1, D], down[p])
    for p in range(2):
        for key in ("b+", "b-", "c+", "c-"):
            two[p][key].wait_recv()
        ready[:, p] = terms[p, c, first[p], second[p]] + in_two[p, 0] + in_two[p, 1]

    last = []
    mine = z // 4
    for k in sorted(range(1, NB), key=lambda k: -min(k, NB - k)):
        last.append(
            send(ready.at[lax.rem(mine + k, NB)], in_last.at[k - 1], along_z(4 * k))
        )
    for copy in last:
        copy.wait_recv()
    summed = ready[mine]
    for k in range(NB - 1):
        summed = summed + in_last[k]
    weight_sum = summed / scale_in

    def largest(values):
        return jnp.max(values, axis=(0, 1), keepdims=True)

    one_row = pl.ds(0, 1)

    def put_peak(n, value):
        peak[n] = jnp.broadcast_to(value, (8, 128))

    top = largest(jnp.max(jnp.abs(weight_sum), axis=0))
    put_peak(0, top)
    send(peak.at[0, one_row], peaks_core.at[one_row], other_core).wait_recv()
    put_peak(1, jnp.maximum(top, peaks_core[0:1, 0:1]))
    plane = [
        send(peak.at[1, one_row], peaks_plane.at[d, one_row], in_plane(d // NY, d % NY))
        for d in range(1, NX * NY)
    ]
    for copy in plane:
        copy.wait_recv()
    best = peak[1, 0:1, :]
    for d in range(1, NX * NY):
        best = jnp.maximum(best, peaks_plane[d, 0:1, :])
    put_peak(2, best)
    way = 1 - 2 * c
    ring = [
        send(peak.at[2, one_row], peaks_z.at[k - 1, one_row], along_z(way * k))
        for k in range(NZ // 2, 0, -1)
    ]
    for copy in ring:
        copy.wait_recv()
    for k in range(NZ // 2):
        best = jnp.maximum(best, peaks_z[k, 0:1, :])
    put_peak(3, best)
    send(peak.at[3, one_row], peaks_end.at[one_row], other_core).wait_recv()
    amax = jnp.maximum(best, peaks_end[0:1, :])

    history = hist_ref[...]
    lane = lax.broadcasted_iota(jnp.int32, (1, 16), 1)
    new_history = jnp.where(lane == 0, amax[:, 0:16], jnp.roll(history, 1, axis=1))
    hist_out[...] = new_history
    out_scale = LIMIT / jnp.max(new_history)
    wq_out[...] = (weight_sum * out_scale).reshape(16, 512)

    for copy in sent:
        copy.wait_send()
    put_ig.wait()


N_SENT = 8 + 12 + 12 + (NB - 1) + 1 + (NX * NY - 1) + NZ // 2 + 1


def shards(out_grad, saved_input, weight, amax_history):
    any_space = pl.BlockSpec(memory_space=pl.ANY)
    vmem = pl.BlockSpec(memory_space=pltpu.VMEM)
    input_grad, weight_q, history = pl.pallas_call(
        kernel,
        out_shape=(
            jax.ShapeDtypeStruct((192, 512), jnp.bfloat16),
            jax.ShapeDtypeStruct((16, 512), F32),
            jax.ShapeDtypeStruct((1, 16), F32),
        ),
        in_specs=[any_space, any_space, any_space, vmem],
        out_specs=[any_space, vmem, vmem],
        scratch_shapes=[
            pltpu.VMEM((192, 4096), jnp.bfloat16),
            pltpu.VMEM((192, 512), jnp.bfloat16),
            pltpu.VMEM((512, 4096), jnp.bfloat16),
            pltpu.VMEM((192, 512), jnp.bfloat16),
            pltpu.VMEM((2, 2, 4, 4, NB, 8, 512), F32),
            pltpu.VMEM((2, 4, 4, NB, 8, 512), F32),
            pltpu.VMEM((2, 2, 2, NB, 8, 512), F32),
            pltpu.VMEM((2, 2, 4, NB, 8, 512), F32),
            pltpu.VMEM((2, 2, NB // 2, 8, 512), F32),
            pltpu.VMEM((2, 2, NB, 8, 512), F32),
            pltpu.VMEM((NB, 2, 8, 512), F32),
            pltpu.VMEM((NB - 1, 2, 8, 512), F32),
            pltpu.VMEM((8, 128), F32),
            pltpu.VMEM((NX * NY, 8, 128), F32),
            pltpu.VMEM((NZ // 2, 8, 128), F32),
            pltpu.VMEM((8, 128), F32),
            pltpu.VMEM((4, 8, 128), F32),
            pltpu.SemaphoreType.DMA((4,)),
            pltpu.SemaphoreType.DMA((N_SENT,)),
            pltpu.SemaphoreType.DMA((N_SENT,)),
        ],
        compiler_params=pltpu.CompilerParams(
            collective_id=0, has_side_effects=True, vmem_limit_bytes=60 * 2**20
        ),
        name="all_steps",
    )(out_grad, saved_input, weight, amax_history.reshape(1, 16))
    return (input_grad, weight_q.T.astype(jnp.bfloat16), history.reshape(16))


def solution(mesh):
    placed = (P("dp", None), P("dp", "tensor"), P("tensor", None), P())
    return jax.shard_map(
        shards,
        mesh=mesh,
        in_specs=placed,
        out_specs=(P("dp", "tensor"), P("tensor", "dp"), P()),
        check_vma=False,
    )
```

time: 704 us -> 118 us (0.17)
  waiting for transfers between devices: 494 us -> 0 us
  blocking collectives: 177 us -> 0 us
  Pallas kernels: 0 us -> 113 us
  between operations: 16.1 us -> 0.64 us
  other arithmetic: 10.4 us -> 1.37 us
    reduce_scatter x1 -> x0, waiting for transfers between devices: 494 us -> none  [shards(): lax.psum_scatter(quantize(transposed_term(out_grad, saved_input), scale_i...]
    pmax x1 -> x0, blocking collectives: 177 us -> none  [shards(): amax = lax.pmax(local_peak, ('dp', 'tensor'))]
    pallas_call x0 -> x1, Pallas kernels: none -> 113 us  [shards(): pl.pallas_call(kernel, out_shape=(jax.ShapeDtypeStruct((192, 512), jnp.bf...]
  transfers between devices with their start and end apart: 1 -> 0, of which waited for: 1 -> 0; matrix products, arithmetic and copies ran while one was open for 1% -> 0% of each run, Pallas kernels for 0% -> 0%
where the time goes in v1:
time: 118 us
  Pallas kernels  113 us (96%)
  local copies, waits for them, and re-layouts  2.76 us (2%)
  other arithmetic  1.37 us (1%)
    pallas_call x1, Pallas kernels, shards(): pl.pallas_call(kernel, out_shape=(jax.ShapeDtypeStruct((192, 512), jnp.bf...  113 us
    unnamed x2, local copies, waits for them, and re-layouts  2.76 us

profile of v1, /device:TPU:1, one launch (start us, length us, event | category | flops | bytes accessed | tf_op | source)
XLA Modules:
  0.0 118.1 jit_solution(10465031925335972720)
XLA Ops:
  0.6 113.4 %all_steps.1 = (bf16[192,512]{1,0:T(8,128)(2,1)}, f32[16,512]{1,0:T(8,128)}, f32[1,16]{1,0:T(1,128)}) custom-call(bf16[192,4096]{1,0:T(8,128)(2,1)} %og_hbm.1, bf16[192,512]{1,0:T(8,128)(2,1)} %si_hbm.1, bf16[512,4096]{1,0:T(8,128)(2,1)} %w_hbm.1, f32[1,16]{1,0:T(1,128)} %bitcast.4), custom_call_target="tpu_custom_call" | custom-call | tf_op jit(solution)/shard_map/all_steps/pallas_call | solution.py:264
  114.0 1.4 %convert_bitcast_fusion = bf16[512,16]{0,1:T(8,128)(2,1)} fusion(f32[16,512]{1,0:T(8,128)} %get-tuple-element.7), kind=kLoop, calls=%fused_computation | loop fusion | flops 8192 | bytes 49152 | tf_op jit(solution)/shard_map/convert_element_type | solution.py:300
  115.4 1.6 %copy.9 = bf16[192,512]{1,0:T(8,128)(2,1)} copy(bf16[192,512]{1,0:T(8,128)(2,1)} %get-tuple-element.12) | data formatting | bytes 393216
  117.0 1.1 copy.10

commit v2 on v1

v2 whole, which is shorter than its diff:
```python
import jax
import jax.numpy as jnp
from jax import lax
from jax.experimental import pallas as pl
from jax.experimental.pallas import tpu as pltpu
from jax.sharding import PartitionSpec as P

LIMIT = 8.0
MESH = pl.DeviceIdType.MESH
NX, NZ, NY = 4, 32, 4
NB = NZ // 4
F32, BF16 = jnp.float32, jnp.bfloat16
ORDER = (2, 1, 3, 0)
PLACE = {k: n for n, k in enumerate(ORDER)}
N_SENT = 5 + 12 + 12 + 1 + (NX * NY - 1) + NZ // 2 + 1


def kernel(
    og_hbm, si_hbm, w_hbm, hist_ref,
    ig_out, wq_out, hist_out,
    og, si, w, ig, si_sent, og_sent, si_core, og_core,
    terms, pass_one, in_one, pass_two, in_two, ready, relay, in_last,
    peaks_core, peaks_plane, peaks_z, peaks_end, peak,
    local_sem, send_sem, recv_sem, last_send, last_recv, relay_sem, hello,
):
    dp, y = lax.axis_index("dp"), lax.axis_index("tensor")
    x, z, c = dp // (2 * NZ), lax.rem(dp // 2, NZ), lax.rem(dp, 2)
    zc, zb = lax.rem(z, 4), z // 4

    def device(x, y, z, c):
        return ((x * NZ + z) * 2 + c, y)

    def along_x(d):
        return device(lax.rem(x + d + NX, NX), y, z, c)

    def along_y(d):
        return device(x, lax.rem(y + d + NY, NY), z, c)

    def along_z(d, core=None):
        return device(x, y, lax.rem(z + d + NZ, NZ), c if core is None else core)

    def in_plane(dx, dy):
        return device(lax.rem(x + dx, NX), lax.rem(y + dy, NY), z, c)

    other_core = device(x, y, z, 1 - c)
    sides = [along_x(1), along_x(-1), along_y(1), along_y(-1)]

    def signal(sem, devices):
        for to in devices:
            pl.semaphore_signal(sem, inc=1, device_id=to, device_id_type=MESH)

    barrier = pltpu.get_barrier_semaphore()
    near = [other_core, along_z(1), along_z(-1)] + sides
    signal(barrier, near)
    rounds = [
        sides + [along_z(1), along_z(-1)],
        sides + [along_z(2), along_z(-2)],
        sides + [along_z(4), along_z(-4)],
        [along_z(8), along_z(-8)],
    ]

    def say(n):
        signal(hello.at[n], rounds[n])

    def hear(n):
        pl.semaphore_wait(hello.at[n], len(rounds[n]))

    get_og = pltpu.make_async_copy(og_hbm, og, local_sem.at[0])
    get_si = pltpu.make_async_copy(si_hbm, si, local_sem.at[1])
    get_w = pltpu.make_async_copy(w_hbm, w, local_sem.at[2])
    get_si.start()
    get_og.start()
    get_w.start()

    used = [0]
    sent = []

    def send(src, dst, to):
        n = used[0]
        used[0] += 1
        copy = pltpu.make_async_remote_copy(
            src_ref=src, dst_ref=dst, send_sem=send_sem.at[n], recv_sem=recv_sem.at[n],
            device_id=to, device_id_type=MESH,
        )
        copy.start()
        sent.append(copy)
        return copy

    scale_in = LIMIT / jnp.max(hist_ref[...])

    def group(at, i, core):
        return pl.ds(pl.multiple_of(at * 1024 + i * 256 + core * 128, 128), 128)

    get_si.wait()
    si_sent[...] = si[...].astype(F32)
    get_og.wait()
    for n, k in enumerate(ORDER):
        for i in range(4):
            og_sent[n, :, i * 128 : i * 128 + 128] = og[
                :, group(lax.rem(x + k, 4), i, 1 - c)
            ].astype(F32)
        if n == 0:
            pl.semaphore_wait(barrier, len(near))
            si_copy = send(si_sent, si_core, other_core)
            og_copies = []
        og_copies.append(send(og_sent.at[n], og_core.at[n], other_core))
    say(0)

    def quantized(grads, inputs):
        term = lax.dot_general(
            grads, inputs, (((0,), (0,)), ((), ())), preferred_element_type=F32
        )
        return jnp.clip(term * scale_in, -LIMIT, LIMIT).astype(BF16).astype(F32)

    def pieces(at, n, first):
        for i in range(2):
            for j in range(4):
                for core in range(2):
                    row = i * 128 + j * 32 + core * 16
                    yield (0, at, j, first + i, core), row
                    yield (1, j, n, first + i, core), row + 8

    def own_tile(n, k):
        at = lax.rem(x + k, 4)

        @pl.loop(0, 2)
        def _(s):
            grads = jnp.concatenate(
                [og[:, group(at, 2 * s, c)], og[:, group(at, 2 * s + 1, c)]], axis=1
            )
            quant = quantized(grads, si[...])
            for where, row in pieces(at, n, 2 * s):
                terms[where] = quant[row : row + 8]

    def other_tile(n, k):
        at = lax.rem(x + k, 4)
        og_copies[n].wait_recv()

        @pl.loop(0, 2)
        def _(s):
            columns = pl.ds(pl.multiple_of(s * 256, 256), 256)
            quant = quantized(og_core[n, :, columns].astype(BF16), si_core[...].astype(BF16))
            for where, row in pieces(at, n, 2 * s):
                terms[where] += quant[row : row + 8]

    @pl.loop(0, 4)
    def _(n):
        own_tile(n, jnp.where(n == 0, 2, jnp.where(n == 1, 1, jnp.where(n == 2, 3, 0))))

    hear(0)
    say(1)
    si_copy.wait_recv()

    A, B = pl.ds(0, 2), pl.ds(2, 2)
    plus = (along_x(1), along_z(1))
    minus = (along_x(-1), along_z(-1))
    first = (x, zc)

    def unit(p, k):
        return terms.at[p, lax.rem(first[p] + k, 4)]

    one = [{}, {}]
    other_tile(0, 2)
    one[0]["a+"] = send(unit(0, 2).at[A], pass_one.at[0, 0], plus[0])
    one[0]["a-"] = send(unit(0, 2).at[B], pass_one.at[0, 1], minus[0])
    other_tile(1, 1)
    one[1]["a+"] = send(unit(1, 2).at[A], pass_one.at[1, 0], plus[1])
    one[0]["b+"] = send(unit(0, 1).at[B], in_one.at[0, 0, B], plus[0])
    one[1]["b-"] = send(unit(1, 3).at[A], in_one.at[1, 1, A], minus[1])
    other_tile(2, 3)
    one[0]["b-"] = send(unit(0, 3).at[A], in_one.at[0, 1, A], minus[0])
    other_tile(3, 0)
    one[1]["a-"] = send(unit(1, 2).at[B], pass_one.at[1, 1], minus[1])
    one[1]["b+"] = send(unit(1, 1).at[B], in_one.at[1, 0, B], plus[1])
    hear(1)
    say(2)

    def pass_on(p, k, half, at, key_in, key_out, to):
        one[p][key_in].wait_recv()
        m = lax.rem(first[p] + k, 4)
        terms[p, m, half] += pass_one[p, at]
        one[p][key_out] = send(terms.at[p, m, half], in_one.at[p, at, half], to)

    pass_on(0, 1, A, 0, "a+", "c+", plus[0])
    pass_on(0, 3, B, 1, "a-", "c-", minus[0])
    pass_on(1, 1, A, 0, "a+", "c+", plus[1])
    pass_on(1, 3, B, 1, "a-", "c-", minus[1])

    get_w.wait()

    @pl.loop(0, 2)
    def _(i):
        rows = pl.ds(pl.multiple_of(i * 256, 256), 256)
        ig[:, rows] = lax.dot_general(
            og[...], w[rows, :], (((1,), (1,)), ((), ())), preferred_element_type=F32
        ).astype(BF16)

    put_ig = pltpu.make_async_copy(ig, ig_out, local_sem.at[3])
    put_ig.start()
    hear(2)
    say(3)

    C, D = pl.ds(0, 2), pl.ds(2, 2)
    two = [{}, {}]
    up, down = (plus[1], plus[0]), (minus[1], minus[0])

    def second(p, k):
        return lax.rem(zc + k, 4) if p == 0 else PLACE[k]

    for p in range(2):
        for key in ("b+", "b-", "c+", "c-"):
            one[p][key].wait_recv()
        m = first[p]

        def total(k):
            q = second(p, k)
            terms[p, m, q] += in_one[p, 0, q] + in_one[p, 1, q]
            return terms.at[p, m, q]

        far = total(2)
        two[p]["a+"] = send(far.at[C], pass_two.at[p, 0], up[p])
        two[p]["a-"] = send(far.at[D], pass_two.at[p, 1], down[p])
        two[p]["b+"] = send(total(1).at[D], in_two.at[p, 0, D], up[p])
        two[p]["b-"] = send(total(3).at[C], in_two.at[p, 1, C], down[p])
        total(0)
    for p in range(2):
        m = first[p]
        for key, out, k, half, at, to in (
            ("a+", "c+", 1, C, 0, up[p]),
            ("a-", "c-", 3, D, 1, down[p]),
        ):
            q = second(p, k)
            two[p][key].wait_recv()
            terms[p, m, q, half] += pass_two[p, at]
            two[p][out] = send(terms.at[p, m, q, half], in_two.at[p, at, half], to)
    for p in range(2):
        for key in ("b+", "b-", "c+", "c-"):
            two[p][key].wait_recv()
        ready[:, p] = terms[p, first[p], second(p, 0)] + in_two[p, 0] + in_two[p, 1]
    hear(3)

    even = lax.rem(zb, 2) == c

    def block(k):
        return lax.rem(zb + k, NB) // 2

    def last_copy(n, src, dst, recv, to):
        return pltpu.make_async_remote_copy(
            src_ref=src, dst_ref=dst, send_sem=last_send.at[n], recv_sem=recv,
            device_id=to, device_id_type=MESH,
        )

    def whole(n, k, core):
        return last_copy(
            n, ready.at[block(k), :, core], in_last.at[k], last_recv.at[k], along_z(4 * k, core)
        )

    def half(n, k, p, core):
        return last_copy(
            n, ready.at[block(k), p, core], in_last.at[k, p], last_recv.at[k if p == 0 else 8 + k],
            along_z(4 * k, core),
        )

    def to_relay(n, p):
        return last_copy(
            n, ready.at[block(4), p], relay.at[p], relay_sem.at[p], along_z(4 if p == 0 else -4)
        )

    def even_copies():
        return [
            to_relay(0, 0), to_relay(1, 1),
            whole(2, 2, 0), whole(3, 6, 0), whole(4, 2, 1), whole(5, 6, 1),
            last_copy(6, ready.at[block(0), :, 1 - c], in_last.at[0], last_recv.at[0], other_core),
        ]

    def odd_copies():
        return [
            half(0, 3, 1, 0), half(1, 5, 0, 0), half(2, 3, 1, 1), half(3, 5, 0, 1),
            whole(4, 1, 0), whole(5, 7, 0), whole(6, 1, 1), whole(7, 7, 1),
        ]

    def odd_passed(p):
        k = 3 if p == 0 else 5
        return [half(8 + 2 * p, k, p, 0), half(9 + 2 * p, k, p, 1)]

    @pl.when(even)
    def _():
        for copy in even_copies():
            copy.start()
        in_last[0] = ready[zb // 2, :, c]

    @pl.when(jnp.logical_not(even))
    def _():
        for copy in odd_copies():
            copy.start()
        for p, k in ((0, 3), (1, 5)):
            to_relay(0, p).wait_recv()
            ready[block(k), p] += relay[p]
            for copy in odd_passed(p):
                copy.start()
        last_copy(0, in_last.at[0], in_last.at[0], last_recv.at[0], other_core).wait_recv()

    summed = in_last[0]
    for k in (1, 7, 2, 6):
        whole(0, k, 0).wait_recv()
        summed = summed + in_last[k]
    for k in (3, 5):
        for p in range(2):
            half(0, k, p, 0).wait_recv()
        summed = summed + in_last[k]
    weight_sum = summed / scale_in

    one_row = pl.ds(0, 1)

    def put_peak(n, value):
        peak[n, 0:1, :] = value

    top = jnp.max(jnp.max(jnp.abs(weight_sum), axis=0), axis=0, keepdims=True)
    best = top[:, 0:128]
    for i in range(1, 4):
        best = jnp.maximum(best, top[:, i * 128 : i * 128 + 128])
    put_peak(0, best)
    send(peak.at[0, one_row], peaks_core.at[one_row], other_core).wait_recv()
    best = jnp.maximum(best, peaks_core[0:1, :])
    put_peak(1, best)
    plane = [
        send(peak.at[1, one_row], peaks_plane.at[d, one_row], in_plane(d // NY, d % NY))
        for d in range(1, NX * NY)
    ]
    for d, copy in enumerate(plane, 1):
        copy.wait_recv()
        best = jnp.maximum(best, peaks_plane[d, 0:1, :])
    put_peak(2, best)
    way = 1 - 2 * c
    ring = [
        send(peak.at[2, one_row], peaks_z.at[k - 1, one_row], along_z(way * k))
        for k in range(NZ // 2, 0, -1)
    ]
    for k, copy in zip(range(NZ // 2, 0, -1), ring):
        copy.wait_recv()
        best = jnp.maximum(best, peaks_z[k - 1, 0:1, :])
    put_peak(3, best)
    send(peak.at[3, one_row], peaks_end.at[one_row], other_core).wait_recv()
    amax = jnp.max(jnp.maximum(best, peaks_end[0:1, :]), axis=1, keepdims=True)

    lane = lax.broadcasted_iota(jnp.int32, (1, 16), 1)
    new_history = jnp.where(lane == 0, amax, jnp.roll(hist_ref[...], 1, axis=1))
    hist_out[...] = new_history
    out_scale = LIMIT / jnp.max(new_history)
    wq_out[...] = (weight_sum * out_scale).reshape(16, 512)

    for copy in sent:
        copy.wait_send()

    @pl.when(even)
    def _():
        for copy in even_copies():
            copy.wait_send()

    @pl.when(jnp.logical_not(even))
    def _():
        for copy in odd_copies() + odd_passed(0) + odd_passed(1):
            copy.wait_send()

    put_ig.wait()


def write_out(ig_in, wq_in, hist_in, ig_out, wq_out, hist_out, sem):
    copy = pltpu.make_async_copy(ig_in, ig_out, sem)
    copy.start()
    wq_out[...] = wq_in[...].astype(BF16)
    hist_out[...] = hist_in[...]
    copy.wait()


def shards(out_grad, saved_input, weight, amax_history):
    any_space = pl.BlockSpec(memory_space=pl.ANY)
    vmem = pl.BlockSpec(memory_space=pltpu.VMEM)
    part = (8, 512)
    input_grad, weight_q, history = pl.pallas_call(
        kernel,
        out_shape=(
            jax.ShapeDtypeStruct((192, 512), BF16),
            jax.ShapeDtypeStruct((16, 512), F32),
            jax.ShapeDtypeStruct((1, 16), F32),
        ),
        in_specs=[any_space, any_space, any_space, vmem],
        out_specs=[any_space, vmem, vmem],
        scratch_shapes=[
            pltpu.VMEM((192, 4096), BF16),
            pltpu.VMEM((192, 512), BF16),
            pltpu.VMEM((512, 4096), BF16),
            pltpu.VMEM((192, 512), BF16),
            pltpu.VMEM((192, 512), F32),
            pltpu.VMEM((4, 192, 512), F32),
            pltpu.VMEM((192, 512), F32),
            pltpu.VMEM((4, 192, 512), F32),
            pltpu.VMEM((2, 4, 4, 4, 2) + part, F32),
            pltpu.VMEM((2, 2, 2, 4, 2) + part, F32),
            pltpu.VMEM((2, 2, 4, 4, 2) + part, F32),
            pltpu.VMEM((2, 2, 2, 2) + part, F32),
            pltpu.VMEM((2, 2, 4, 2) + part, F32),
            pltpu.VMEM((4, 2, 2) + part, F32),
            pltpu.VMEM((2, 2) + part, F32),
            pltpu.VMEM((NB, 2) + part, F32),
            pltpu.VMEM((8, 128), F32),
            pltpu.VMEM((NX * NY, 8, 128), F32),
            pltpu.VMEM((NZ // 2, 8, 128), F32),
            pltpu.VMEM((8, 128), F32),
            pltpu.VMEM((4, 8, 128), F32),
            pltpu.SemaphoreType.DMA((4,)),
            pltpu.SemaphoreType.DMA((N_SENT,)),
            pltpu.SemaphoreType.DMA((N_SENT,)),
            pltpu.SemaphoreType.DMA((12,)),
            pltpu.SemaphoreType.DMA((16,)),
            pltpu.SemaphoreType.DMA((2,)),
            pltpu.SemaphoreType.REGULAR((4,)),
        ],
        compiler_params=pltpu.CompilerParams(
            collective_id=0, has_side_effects=True, vmem_limit_bytes=60 * 2**20
        ),
        name="all_steps",
    )(out_grad, saved_input, weight, amax_history.reshape(1, 16))
    input_grad, weight_q, history = pl.pallas_call(
        write_out,
        out_shape=(
            jax.ShapeDtypeStruct((192, 512), BF16),
            jax.ShapeDtypeStruct((16, 512), BF16),
            jax.ShapeDtypeStruct((1, 16), F32),
        ),
        in_specs=[any_space, vmem, vmem],
        out_specs=[any_space, vmem, vmem],
        scratch_shapes=[pltpu.SemaphoreType.DMA],
        compiler_params=pltpu.CompilerParams(vmem_limit_bytes=60 * 2**20),
        name="write_out",
    )(input_grad, weight_q, history)
    return (input_grad, weight_q.T, history.reshape(16))


def solution(mesh):
    placed = (P("dp", None), P("dp", "tensor"), P("tensor", None), P())
    return jax.shard_map(
        shards,
        mesh=mesh,
        in_specs=placed,
        out_specs=(P("dp", "tensor"), P("tensor", "dp"), P()),
        check_vma=False,
    )
```

time: 118 us -> 108 us (0.915)
  Pallas kernels: 113 us -> 107 us
  local copies, waits for them, and re-layouts: 2.76 us -> 0 us
  other arithmetic: 1.37 us -> 0 us
    pallas_call x1 -> x2, Pallas kernels: 113 us -> 107 us  [the longest x1 98.7 us: shards(): pl.pallas_call(kernel, out_shape=(jax.ShapeDtypeStruct((192, 512), BF16),...]
    unnamed x2 -> x0, local copies, waits for them, and re-layouts: 2.76 us -> none
    convert_element_type x1 -> x0, other arithmetic: 1.37 us -> none  [shards(): return (input_grad, weight_q.T.astype(jnp.bfloat16), history.reshape(16))]
where the time goes in v2:
time: 108 us
  Pallas kernels  107 us (99%)
    pallas_call x1, Pallas kernels, shards(): pl.pallas_call(kernel, out_shape=(jax.ShapeDtypeStruct((192, 512), BF16),...  98.7 us
    pallas_call x1, Pallas kernels, shards(): pl.pallas_call(write_out, out_shape=(jax.ShapeDtypeStruct((192, 512), BF1...  8.43 us

profile of v2, /device:TPU:1, one launch (start us, length us, event | category | flops | bytes accessed | tf_op | source)
XLA Modules:
  0.0 107.8 jit_solution(2289345913990023392)
XLA Ops:
  0.6 98.7 %all_steps.1 = (bf16[192,512]{1,0:T(8,128)(2,1)}, f32[16,512]{1,0:T(8,128)}, f32[1,16]{1,0:T(1,128)}) custom-call(bf16[192,4096]{1,0:T(8,128)(2,1)} %og_hbm.1, bf16[192,512]{1,0:T(8,128)(2,1)} %si_hbm.1, bf16[512,4096]{1,0:T(8,128)(2,1)} %w_hbm.1, f32[1,16]{1,0:T(1,128)} %bitcast.3), custom_call_target="tpu_custom_call" | custom-call | tf_op jit(solution)/shard_map/all_steps/pallas_call | solution.py:380
  99.3 8.4 %write_out.1 = (bf16[192,512]{1,0:T(8,128)(2,1)}, bf16[16,512]{1,0:T(8,128)(2,1)}, f32[1,16]{1,0:T(1,128)}) custom-call(bf16[192,512]{1,0:T(8,128)(2,1)} %get-tuple-element.9.ig_in, f32[16,512]{1,0:T(8,128)} %get-tuple-element.10.wq_in, f32[1,16]{1,0:T(1,128)} %get-tuple-element.11.hist_in), custom_call_target="tpu_custom_call" | custom-call | tf_op jit(solution)/shard_map/write_out/pallas_call | solution.py:424

commit v3 on v2

--- a/solution.py
+++ b/solution.py
@@ -12,15 +12,15 @@
 F32, BF16 = jnp.float32, jnp.bfloat16
 ORDER = (2, 1, 3, 0)
 PLACE = {k: n for n, k in enumerate(ORDER)}
-N_SENT = 5 + 12 + 12 + 1 + (NX * NY - 1) + NZ // 2 + 1
+N_SENT = 5 + 12 + 12 + (2 * NX * NY - 1) + NZ // 2 + 1
 
 
 def kernel(
     og_hbm, si_hbm, w_hbm, hist_ref,
     ig_out, wq_out, hist_out,
-    og, si, w, ig, si_sent, og_sent, si_core, og_core,
-    terms, pass_one, in_one, pass_two, in_two, ready, relay, in_last,
-    peaks_core, peaks_plane, peaks_z, peaks_end, peak,
+    og, si, w, ig, si_sent, og_sent, si_core, og_core, si_other,
+    terms, pass_one, in_one, pass_two, in_two, ready, relay, relay_far, in_last,
+    peaks_plane, peaks_z, peaks_end, peak,
     local_sem, send_sem, recv_sem, last_send, last_recv, relay_sem, hello,
 ):
     dp, y = lax.axis_index("dp"), lax.axis_index("tensor")
@@ -39,8 +39,8 @@
     def along_z(d, core=None):
         return device(x, y, lax.rem(z + d + NZ, NZ), c if core is None else core)
 
-    def in_plane(dx, dy):
-        return device(lax.rem(x + dx, NX), lax.rem(y + dy, NY), z, c)
+    def in_plane(dx, dy, dc):
+        return device(lax.rem(x + dx, NX), lax.rem(y + dy, NY), z, lax.rem(c + dc, 2))
 
     other_core = device(x, y, z, 1 - c)
     sides = [along_x(1), along_x(-1), along_y(1), along_y(-1)]
@@ -65,12 +65,20 @@
     def hear(n):
         pl.semaphore_wait(hello.at[n], len(rounds[n]))
 
-    get_og = pltpu.make_async_copy(og_hbm, og, local_sem.at[0])
-    get_si = pltpu.make_async_copy(si_hbm, si, local_sem.at[1])
-    get_w = pltpu.make_async_copy(w_hbm, w, local_sem.at[2])
+    def columns_of(k):
+        return pl.ds(pl.multiple_of(lax.rem(x + k, 4) * 1024, 1024), 1024)
+
+    get_si = pltpu.make_async_copy(si_hbm, si, local_sem.at[0])
+    get_og = [
+        pltpu.make_async_copy(
+            og_hbm.at[:, columns_of(k)], og.at[:, columns_of(k)], local_sem.at[1 + n]
+        )
+        for n, k in enumerate(ORDER)
+    ]
+    get_w = pltpu.make_async_copy(w_hbm, w, local_sem.at[5])
     get_si.start()
-    get_og.start()
-    get_w.start()
+    for copy in get_og:
+        copy.start()
 
     used = [0]
     sent = []
@@ -93,8 +101,9 @@
 
     get_si.wait()
     si_sent[...] = si[...].astype(F32)
-    get_og.wait()
+    og_copies = []
     for n, k in enumerate(ORDER):
+        get_og[n].wait()
         for i in range(4):
             og_sent[n, :, i * 128 : i * 128 + 128] = og[
                 :, group(lax.rem(x + k, 4), i, 1 - c)
@@ -102,8 +111,8 @@
         if n == 0:
             pl.semaphore_wait(barrier, len(near))
             si_copy = send(si_sent, si_core, other_core)
-            og_copies = []
         og_copies.append(send(og_sent.at[n], og_core.at[n], other_core))
+    get_w.start()
     say(0)
 
     def quantized(grads, inputs):
@@ -134,22 +143,17 @@
 
     def other_tile(n, k):
         at = lax.rem(x + k, 4)
+        if n == 0:
+            si_copy.wait_recv()
+            si_other[...] = si_core[...].astype(BF16)
         og_copies[n].wait_recv()
 
         @pl.loop(0, 2)
         def _(s):
             columns = pl.ds(pl.multiple_of(s * 256, 256), 256)
-            quant = quantized(og_core[n, :, columns].astype(BF16), si_core[...].astype(BF16))
+            quant = quantized(og_core[n, :, columns].astype(BF16), si_other[...])
             for where, row in pieces(at, n, 2 * s):
                 terms[where] += quant[row : row + 8]
-
-    @pl.loop(0, 4)
-    def _(n):
-        own_tile(n, jnp.where(n == 0, 2, jnp.where(n == 1, 1, jnp.where(n == 2, 3, 0))))
-
-    hear(0)
-    say(1)
-    si_copy.wait_recv()
 
     A, B = pl.ds(0, 2), pl.ds(2, 2)
     plus = (along_x(1), along_z(1))
@@ -160,15 +164,21 @@
         return terms.at[p, lax.rem(first[p] + k, 4)]
 
     one = [{}, {}]
+    own_tile(0, 2)
     other_tile(0, 2)
     one[0]["a+"] = send(unit(0, 2).at[A], pass_one.at[0, 0], plus[0])
     one[0]["a-"] = send(unit(0, 2).at[B], pass_one.at[0, 1], minus[0])
+    hear(0)
+    say(1)
+    own_tile(1, 1)
     other_tile(1, 1)
     one[1]["a+"] = send(unit(1, 2).at[A], pass_one.at[1, 0], plus[1])
     one[0]["b+"] = send(unit(0, 1).at[B], in_one.at[0, 0, B], plus[0])
     one[1]["b-"] = send(unit(1, 3).at[A], in_one.at[1, 1, A], minus[1])
+    own_tile(2, 3)
     other_tile(2, 3)
     one[0]["b-"] = send(unit(0, 3).at[A], in_one.at[0, 1, A], minus[0])
+    own_tile(3, 0)
     other_tile(3, 0)
     one[1]["a-"] = send(unit(1, 2).at[B], pass_one.at[1, 1], minus[1])
     one[1]["b+"] = send(unit(1, 1).at[B], in_one.at[1, 0, B], plus[1])
@@ -195,7 +205,7 @@
             og[...], w[rows, :], (((1,), (1,)), ((), ())), preferred_element_type=F32
         ).astype(BF16)
 
-    put_ig = pltpu.make_async_copy(ig, ig_out, local_sem.at[3])
+    put_ig = pltpu.make_async_copy(ig, ig_out, local_sem.at[6])
     put_ig.start()
     hear(2)
     say(3)
@@ -255,59 +265,55 @@
             n, ready.at[block(k), :, core], in_last.at[k], last_recv.at[k], along_z(4 * k, core)
         )
 
-    def half(n, k, p, core):
+    def relay_half(n, p):
         return last_copy(
-            n, ready.at[block(k), p, core], in_last.at[k, p], last_recv.at[k if p == 0 else 8 + k],
-            along_z(4 * k, core),
-        )
-
-    def to_relay(n, p):
+            n, ready.at[block(4), p], relay_far.at[p], relay_sem.at[p], along_z(8 if p == 0 else -8)
+        )
+
+    def relay_whole(n, k):
+        at = 0 if k == 3 else 1
         return last_copy(
-            n, ready.at[block(4), p], relay.at[p], relay_sem.at[p], along_z(4 if p == 0 else -4)
-        )
-
-    def even_copies():
-        return [
-            to_relay(0, 0), to_relay(1, 1),
-            whole(2, 2, 0), whole(3, 6, 0), whole(4, 2, 1), whole(5, 6, 1),
-            last_copy(6, ready.at[block(0), :, 1 - c], in_last.at[0], last_recv.at[0], other_core),
-        ]
+            n, ready.at[block(k)], relay.at[at], relay_sem.at[2 + at], along_z(4 if k == 3 else -4)
+        )
+
+    def even_first():
+        to_core = last_copy(
+            2, ready.at[block(0), :, 1 - c], in_last.at[0], last_recv.at[0], other_core
+        )
+        return [relay_half(0, 0), relay_half(1, 1), to_core]
+
+    def even_then(k):
+        return [whole(1 + k, k, 0), whole(2 + k, k, 1)]
 
     def odd_copies():
         return [
-            half(0, 3, 1, 0), half(1, 5, 0, 0), half(2, 3, 1, 1), half(3, 5, 0, 1),
-            whole(4, 1, 0), whole(5, 7, 0), whole(6, 1, 1), whole(7, 7, 1),
+            relay_whole(0, 3), relay_whole(1, 5),
+            whole(2, 1, 0), whole(3, 7, 0), whole(4, 1, 1), whole(5, 7, 1),
         ]
-
-    def odd_passed(p):
-        k = 3 if p == 0 else 5
-        return [half(8 + 2 * p, k, p, 0), half(9 + 2 * p, k, p, 1)]
 
     @pl.when(even)
     def _():
-        for copy in even_copies():
+        for copy in even_first():
             copy.start()
         in_last[0] = ready[zb // 2, :, c]
+        for p, k in ((0, 2), (1, 6)):
+            relay_whole(0, 3 if p == 0 else 5).wait_recv()
+            ready[block(k)] += relay[p]
+            relay_half(0, p).wait_recv()
+            ready[block(k), p] += relay_far[p]
+            for copy in even_then(k):
+                copy.start()
 
     @pl.when(jnp.logical_not(even))
     def _():
         for copy in odd_copies():
             copy.start()
-        for p, k in ((0, 3), (1, 5)):
-            to_relay(0, p).wait_recv()
-            ready[block(k), p] += relay[p]
-            for copy in odd_passed(p):
-                copy.start()
         last_copy(0, in_last.at[0], in_last.at[0], last_recv.at[0], other_core).wait_recv()
 
     summed = in_last[0]
     for k in (1, 7, 2, 6):
         whole(0, k, 0).wait_recv()
         summed = summed + in_last[k]
-    for k in (3, 5):
-        for p in range(2):
-            half(0, k, p, 0).wait_recv()
-        summed = summed + in_last[k]
     weight_sum = summed / scale_in
 
     one_row = pl.ds(0, 1)
@@ -319,13 +325,10 @@
     best = top[:, 0:128]
     for i in range(1, 4):
         best = jnp.maximum(best, top[:, i * 128 : i * 128 + 128])
-    put_peak(0, best)
-    send(peak.at[0, one_row], peaks_core.at[one_row], other_core).wait_recv()
-    best = jnp.maximum(best, peaks_core[0:1, :])
     put_peak(1, best)
     plane = [
-        send(peak.at[1, one_row], peaks_plane.at[d, one_row], in_plane(d // NY, d % NY))
-        for d in range(1, NX * NY)
+        send(peak.at[1, one_row], peaks_plane.at[d, one_row], in_plane(d // 2 // NY, d // 2 % NY, d % 2))
+        for d in range(1, 2 * NX * NY)
     ]
     for d, copy in enumerate(plane, 1):
         copy.wait_recv()
@@ -354,23 +357,21 @@
 
     @pl.when(even)
     def _():
-        for copy in even_copies():
+        for copy in even_first() + even_then(2) + even_then(6):
             copy.wait_send()
 
     @pl.when(jnp.logical_not(even))
     def _():
-        for copy in odd_copies() + odd_passed(0) + odd_passed(1):
+        for copy in odd_copies():
             copy.wait_send()
 
     put_ig.wait()
 
 
-def write_out(ig_in, wq_in, hist_in, ig_out, wq_out, hist_out, sem):
-    copy = pltpu.make_async_copy(ig_in, ig_out, sem)
-    copy.start()
+def write_out(ig_in, wq_in, hist_in, ig_out, wq_out, hist_out):
+    ig_out[...] = ig_in[...]
     wq_out[...] = wq_in[...].astype(BF16)
     hist_out[...] = hist_in[...]
-    copy.wait()
 
 
 def shards(out_grad, saved_input, weight, amax_history):
@@ -395,25 +396,26 @@
             pltpu.VMEM((4, 192, 512), F32),
             pltpu.VMEM((192, 512), F32),
             pltpu.VMEM((4, 192, 512), F32),
+            pltpu.VMEM((192, 512), BF16),
             pltpu.VMEM((2, 4, 4, 4, 2) + part, F32),
             pltpu.VMEM((2, 2, 2, 4, 2) + part, F32),
             pltpu.VMEM((2, 2, 4, 4, 2) + part, F32),
             pltpu.VMEM((2, 2, 2, 2) + part, F32),
             pltpu.VMEM((2, 2, 4, 2) + part, F32),
             pltpu.VMEM((4, 2, 2) + part, F32),
+            pltpu.VMEM((2, 2, 2) + part, F32),
             pltpu.VMEM((2, 2) + part, F32),
             pltpu.VMEM((NB, 2) + part, F32),
-            pltpu.VMEM((8, 128), F32),
-            pltpu.VMEM((NX * NY, 8, 128), F32),
+            pltpu.VMEM((2 * NX * NY, 8, 128), F32),
             pltpu.VMEM((NZ // 2, 8, 128), F32),
             pltpu.VMEM((8, 128), F32),
             pltpu.VMEM((4, 8, 128), F32),
-            pltpu.SemaphoreType.DMA((4,)),
+            pltpu.SemaphoreType.DMA((7,)),
             pltpu.SemaphoreType.DMA((N_SENT,)),
             pltpu.SemaphoreType.DMA((N_SENT,)),
-            pltpu.SemaphoreType.DMA((12,)),
-            pltpu.SemaphoreType.DMA((16,)),
-            pltpu.SemaphoreType.DMA((2,)),
+            pltpu.SemaphoreType.DMA((9,)),
+            pltpu.SemaphoreType.DMA((NB,)),
+            pltpu.SemaphoreType.DMA((4,)),
             pltpu.SemaphoreType.REGULAR((4,)),
         ],
         compiler_params=pltpu.CompilerParams(
@@ -428,9 +430,8 @@
             jax.ShapeDtypeStruct((16, 512), BF16),
             jax.ShapeDtypeStruct((1, 16), F32),
         ),
-        in_specs=[any_space, vmem, vmem],
-        out_specs=[any_space, vmem, vmem],
-        scratch_shapes=[pltpu.SemaphoreType.DMA],
+        in_specs=[vmem, vmem, vmem],
+        out_specs=[vmem, vmem, vmem],
         compiler_params=pltpu.CompilerParams(vmem_limit_bytes=60 * 2**20),
         name="write_out",
     )(input_grad, weight_q, history)

time: 108 us -> 97.9 us (0.906)
  Pallas kernels: 107 us -> 97.1 us
    pallas_call x1, Pallas kernels: 8.43 us -> 1.64 us  [shards(): pl.pallas_call(write_out, out_shape=(jax.ShapeDtypeStruct((192, 512), BF1...]
    pallas_call x1, Pallas kernels: 98.7 us -> 95.4 us  [shards(): pl.pallas_call(kernel, out_shape=(jax.ShapeDtypeStruct((192, 512), BF16),...]
where the time goes in v3:
time: 97.9 us; the launch traced here: 97.7 us
  Pallas kernels  97.1 us (99%)
    pallas_call x1, Pallas kernels, shards(): pl.pallas_call(kernel, out_shape=(jax.ShapeDtypeStruct((192, 512), BF16),...  95.4 us

profile of v3, /device:TPU:1, one launch (start us, length us, event | category | flops | bytes accessed | tf_op | source)
XLA Modules:
  0.0 97.7 jit_solution(4937719822969489366)
XLA Ops:
  0.6 95.4 %all_steps.1 = (bf16[192,512]{1,0:T(8,128)(2,1)}, f32[16,512]{1,0:T(8,128)}, f32[1,16]{1,0:T(1,128)}) custom-call(bf16[192,4096]{1,0:T(8,128)(2,1)} %og_hbm.1, bf16[192,512]{1,0:T(8,128)(2,1)} %si_hbm.1, bf16[512,4096]{1,0:T(8,128)(2,1)} %w_hbm.1, f32[1,16]{1,0:T(1,128)} %bitcast.3), custom_call_target="tpu_custom_call" | custom-call | tf_op jit(solution)/shard_map/all_steps/pallas_call | solution.py:381
  96.0 1.6 %write_out.1 = (bf16[192,512]{1,0:T(8,128)(2,1)}, bf16[16,512]{1,0:T(8,128)(2,1)}, f32[1,16]{1,0:T(1,128)}) custom-call(bf16[192,512]{1,0:T(8,128)(2,1)} %get-tuple-element.9.ig_in, f32[16,512]{1,0:T(8,128)} %get-tuple-element.10.wq_in, f32[1,16]{1,0:T(1,128)} %get-tuple-element.11.hist_in), custom_call_target="tpu_custom_call" | custom-call | tf_op jit(solution)/shard_map/write_out/pallas_call | solution.py:426

commit v4 on v3

--- a/solution.py
+++ b/solution.py
@@ -93,6 +93,10 @@
         copy.start()
         sent.append(copy)
         return copy
+
+    def left(copy):
+        copy.wait_send()
+        sent[:] = [other for other in sent if other is not copy]
 
     scale_in = LIMIT / jnp.max(hist_ref[...])
 
@@ -173,15 +177,11 @@
     own_tile(1, 1)
     other_tile(1, 1)
     one[1]["a+"] = send(unit(1, 2).at[A], pass_one.at[1, 0], plus[1])
-    one[0]["b+"] = send(unit(0, 1).at[B], in_one.at[0, 0, B], plus[0])
-    one[1]["b-"] = send(unit(1, 3).at[A], in_one.at[1, 1, A], minus[1])
     own_tile(2, 3)
     other_tile(2, 3)
-    one[0]["b-"] = send(unit(0, 3).at[A], in_one.at[0, 1, A], minus[0])
     own_tile(3, 0)
     other_tile(3, 0)
     one[1]["a-"] = send(unit(1, 2).at[B], pass_one.at[1, 1], minus[1])
-    one[1]["b+"] = send(unit(1, 1).at[B], in_one.at[1, 0, B], plus[1])
     hear(1)
     say(2)
 
@@ -191,8 +191,19 @@
         terms[p, m, half] += pass_one[p, at]
         one[p][key_out] = send(terms.at[p, m, half], in_one.at[p, at, half], to)
 
+    def direct(p, sign):
+        left(one[p]["a" + sign])
+        if sign == "+":
+            one[p]["b+"] = send(unit(p, 1).at[B], in_one.at[p, 0, B], plus[p])
+        else:
+            one[p]["b-"] = send(unit(p, 3).at[A], in_one.at[p, 1, A], minus[p])
+
+    direct(0, "+")
+    direct(0, "-")
+    direct(1, "+")
     pass_on(0, 1, A, 0, "a+", "c+", plus[0])
     pass_on(0, 3, B, 1, "a-", "c-", minus[0])
+    direct(1, "-")
     pass_on(1, 1, A, 0, "a+", "c+", plus[1])
     pass_on(1, 3, B, 1, "a-", "c-", minus[1])
 
@@ -217,22 +228,24 @@
     def second(p, k):
         return lax.rem(zc + k, 4) if p == 0 else PLACE[k]
 
+    def total(p, k):
+        m, q = first[p], second(p, k)
+        terms[p, m, q] += in_one[p, 0, q] + in_one[p, 1, q]
+        return terms.at[p, m, q]
+
     for p in range(2):
         for key in ("b+", "b-", "c+", "c-"):
             one[p][key].wait_recv()
-        m = first[p]
-
-        def total(k):
-            q = second(p, k)
-            terms[p, m, q] += in_one[p, 0, q] + in_one[p, 1, q]
-            return terms.at[p, m, q]
-
-        far = total(2)
+        far = total(p, 2)
         two[p]["a+"] = send(far.at[C], pass_two.at[p, 0], up[p])
         two[p]["a-"] = send(far.at[D], pass_two.at[p, 1], down[p])
-        two[p]["b+"] = send(total(1).at[D], in_two.at[p, 0, D], up[p])
-        two[p]["b-"] = send(total(3).at[C], in_two.at[p, 1, C], down[p])
-        total(0)
+    for p in range(2):
+        near_up, near_down = total(p, 1), total(p, 3)
+        left(two[p]["a+"])
+        two[p]["b+"] = send(near_up.at[D], in_two.at[p, 0, D], up[p])
+        left(two[p]["a-"])
+        two[p]["b-"] = send(near_down.at[C], in_two.at[p, 1, C], down[p])
+        total(p, 0)
     for p in range(2):
         m = first[p]
         for key, out, k, half, at, to in (
@@ -285,11 +298,11 @@
     def even_then(k):
         return [whole(1 + k, k, 0), whole(2 + k, k, 1)]
 
-    def odd_copies():
-        return [
-            relay_whole(0, 3), relay_whole(1, 5),
-            whole(2, 1, 0), whole(3, 7, 0), whole(4, 1, 1), whole(5, 7, 1),
-        ]
+    def odd_first():
+        return [relay_whole(0, 3), relay_whole(1, 5)]
+
+    def odd_then():
+        return [whole(2, 1, 0), whole(3, 7, 0), whole(4, 1, 1), whole(5, 7, 1)]
 
     @pl.when(even)
     def _():
@@ -306,7 +319,11 @@
 
     @pl.when(jnp.logical_not(even))
     def _():
-        for copy in odd_copies():
+        for copy in odd_first():
+            copy.start()
+        for copy in odd_first():
+            copy.wait_send()
+        for copy in odd_then():
             copy.start()
         last_copy(0, in_last.at[0], in_last.at[0], last_recv.at[0], other_core).wait_recv()
 
@@ -362,7 +379,7 @@
 
     @pl.when(jnp.logical_not(even))
     def _():
-        for copy in odd_copies():
+        for copy in odd_then():
             copy.wait_send()
 
     put_ig.wait()

time: 97.9 us -> 101 us (1.032)
  Pallas kernels: 97.1 us -> 101 us
    pallas_call x1, Pallas kernels: 95.4 us -> 99 us  [shards(): pl.pallas_call(kernel, out_shape=(jax.ShapeDtypeStruct((192, 512), BF16),...]
where the time goes in v4:
time: 101 us
  Pallas kernels  101 us (100%)
    pallas_call x1, Pallas kernels, shards(): pl.pallas_call(kernel, out_shape=(jax.ShapeDtypeStruct((192, 512), BF16),...  99 us

profile of v4, /device:TPU:1, one launch (start us, length us, event | category | flops | bytes accessed | tf_op | source)
XLA Modules:
  0.0 101.3 jit_solution(16321286551808695738)
XLA Ops:
  0.6 99.0 %all_steps.1 = (bf16[192,512]{1,0:T(8,128)(2,1)}, f32[16,512]{1,0:T(8,128)}, f32[1,16]{1,0:T(1,128)}) custom-call(bf16[192,4096]{1,0:T(8,128)(2,1)} %og_hbm.1, bf16[192,512]{1,0:T(8,128)(2,1)} %si_hbm.1, bf16[512,4096]{1,0:T(8,128)(2,1)} %w_hbm.1, f32[1,16]{1,0:T(1,128)} %bitcast.3), custom_call_target="tpu_custom_call" | custom-call | tf_op jit(solution)/shard_map/all_steps/pallas_call | solution.py:398
  99.6 1.6 %write_out.1 = (bf16[192,512]{1,0:T(8,128)(2,1)}, bf16[16,512]{1,0:T(8,128)(2,1)}, f32[1,16]{1,0:T(1,128)}) custom-call(bf16[192,512]{1,0:T(8,128)(2,1)} %get-tuple-element.9.ig_in, f32[16,512]{1,0:T(8,128)} %get-tuple-element.10.wq_in, f32[1,16]{1,0:T(1,128)} %get-tuple-element.11.hist_in), custom_call_target="tpu_custom_call" | custom-call | tf_op jit(solution)/shard_map/write_out/pallas_call | solution.py:443

commit v5 on v3

--- a/solution.py
+++ b/solution.py
@@ -12,7 +12,7 @@
 F32, BF16 = jnp.float32, jnp.bfloat16
 ORDER = (2, 1, 3, 0)
 PLACE = {k: n for n, k in enumerate(ORDER)}
-N_SENT = 5 + 12 + 12 + (2 * NX * NY - 1) + NZ // 2 + 1
+N_SENT = 5 + 12 + 12 + (2 * NX * NY - 1) + (NZ - 1)
 
 
 def kernel(
@@ -20,7 +20,7 @@
     ig_out, wq_out, hist_out,
     og, si, w, ig, si_sent, og_sent, si_core, og_core, si_other,
     terms, pass_one, in_one, pass_two, in_two, ready, relay, relay_far, in_last,
-    peaks_plane, peaks_z, peaks_end, peak,
+    peaks_plane, peaks_z, peak,
     local_sem, send_sem, recv_sem, last_send, last_recv, relay_sem, hello,
 ):
     dp, y = lax.axis_index("dp"), lax.axis_index("tensor")
@@ -217,7 +217,7 @@
     def second(p, k):
         return lax.rem(zc + k, 4) if p == 0 else PLACE[k]
 
-    for p in range(2):
+    def second_start(p):
         for key in ("b+", "b-", "c+", "c-"):
             one[p][key].wait_recv()
         m = first[p]
@@ -233,7 +233,8 @@
         two[p]["b+"] = send(total(1).at[D], in_two.at[p, 0, D], up[p])
         two[p]["b-"] = send(total(3).at[C], in_two.at[p, 1, C], down[p])
         total(0)
-    for p in range(2):
+
+    def second_pass(p):
         m = first[p]
         for key, out, k, half, at, to in (
             ("a+", "c+", 1, C, 0, up[p]),
@@ -243,13 +244,14 @@
             two[p][key].wait_recv()
             terms[p, m, q, half] += pass_two[p, at]
             two[p][out] = send(terms.at[p, m, q, half], in_two.at[p, at, half], to)
-    for p in range(2):
+
+    def second_end(p):
         for key in ("b+", "b-", "c+", "c-"):
             two[p][key].wait_recv()
         ready[:, p] = terms[p, first[p], second(p, 0)] + in_two[p, 0] + in_two[p, 1]
-    hear(3)
 
     even = lax.rem(zb, 2) == c
+    odd = jnp.logical_not(even)
 
     def block(k):
         return lax.rem(zb + k, NB) // 2
@@ -260,91 +262,119 @@
             device_id=to, device_id_type=MESH,
         )
 
-    def whole(n, k, core):
+    def piece(n, k, p, core):
         return last_copy(
-            n, ready.at[block(k), :, core], in_last.at[k], last_recv.at[k], along_z(4 * k, core)
-        )
-
-    def relay_half(n, p):
+            n, ready.at[block(k), p, core], in_last.at[k, p], last_recv.at[2 * k + p],
+            along_z(4 * k, core),
+        )
+
+    def to_core(n, p):
         return last_copy(
-            n, ready.at[block(4), p], relay_far.at[p], relay_sem.at[p], along_z(8 if p == 0 else -8)
-        )
-
-    def relay_whole(n, k):
-        at = 0 if k == 3 else 1
+            n, ready.at[block(0), p, 1 - c], in_last.at[0, p], last_recv.at[p], other_core
+        )
+
+    def relay_half(n, p, at):
         return last_copy(
-            n, ready.at[block(k)], relay.at[at], relay_sem.at[2 + at], along_z(4 if k == 3 else -4)
-        )
-
-    def even_first():
-        to_core = last_copy(
-            2, ready.at[block(0), :, 1 - c], in_last.at[0], last_recv.at[0], other_core
-        )
-        return [relay_half(0, 0), relay_half(1, 1), to_core]
-
-    def even_then(k):
-        return [whole(1 + k, k, 0), whole(2 + k, k, 1)]
-
-    def odd_copies():
+            n, ready.at[block(4), p, at], relay_far.at[p, at], relay_sem.at[2 * p + at],
+            along_z(8 if at == 0 else -8),
+        )
+
+    def relay_whole(n, p, at):
+        return last_copy(
+            n, ready.at[block(3 if at == 0 else 5), p], relay.at[p, at],
+            relay_sem.at[4 + 2 * p + at], along_z(4 if at == 0 else -4),
+        )
+
+    def even_first(p):
+        return [relay_half(8 * p, p, 0), relay_half(8 * p + 1, p, 1), to_core(8 * p + 2, p)]
+
+    def even_then(p, k):
+        n = 8 * p + (3 if k == 2 else 5)
+        return [piece(n, k, p, 0), piece(n + 1, k, p, 1)]
+
+    def odd_copies(p):
+        n = 8 * p
         return [
-            relay_whole(0, 3), relay_whole(1, 5),
-            whole(2, 1, 0), whole(3, 7, 0), whole(4, 1, 1), whole(5, 7, 1),
+            relay_whole(n, p, 0), relay_whole(n + 1, p, 1), piece(n + 2, 1, p, 0),
+            piece(n + 3, 7, p, 0), piece(n + 4, 1, p, 1), piece(n + 5, 7, p, 1),
         ]
 
-    @pl.when(even)
-    def _():
-        for copy in even_first():
-            copy.start()
-        in_last[0] = ready[zb // 2, :, c]
-        for p, k in ((0, 2), (1, 6)):
-            relay_whole(0, 3 if p == 0 else 5).wait_recv()
-            ready[block(k)] += relay[p]
-            relay_half(0, p).wait_recv()
-            ready[block(k), p] += relay_far[p]
-            for copy in even_then(k):
+    def last_start(p):
+        @pl.when(even)
+        def _():
+            for copy in even_first(p):
                 copy.start()
-
-    @pl.when(jnp.logical_not(even))
-    def _():
-        for copy in odd_copies():
-            copy.start()
-        last_copy(0, in_last.at[0], in_last.at[0], last_recv.at[0], other_core).wait_recv()
-
+            in_last[0, p] = ready[zb // 2, p, c]
+
+        @pl.when(odd)
+        def _():
+            for copy in odd_copies(p):
+                copy.start()
+
+    def last_pass(p):
+        @pl.when(even)
+        def _():
+            for at, k in ((0, 2), (1, 6)):
+                relay_whole(0, p, at).wait_recv()
+                ready[block(k), p] += relay[p, at]
+                relay_half(0, p, at).wait_recv()
+                ready[block(k), p, at] += relay_far[p, at]
+                for copy in even_then(p, k):
+                    copy.start()
+
+        @pl.when(odd)
+        def _():
+            last_copy(
+                0, in_last.at[0, p], in_last.at[0, p], last_recv.at[p], other_core
+            ).wait_recv()
+
+    second_start(0)
+    second_pass(0)
+    second_start(1)
+    second_end(0)
+    hear(3)
+    last_start(0)
+    second_pass(1)
+    second_end(1)
+    last_start(1)
+    for p in range(2):
+        last_pass(p)
+    for p in range(2):
+        for k in (1, 7, 2, 6):
+            piece(0, k, p, 0).wait_recv()
     summed = in_last[0]
     for k in (1, 7, 2, 6):
-        whole(0, k, 0).wait_recv()
         summed = summed + in_last[k]
     weight_sum = summed / scale_in
 
     one_row = pl.ds(0, 1)
 
-    def put_peak(n, value):
-        peak[n, 0:1, :] = value
-
+    def largest(best, at, slots, devices):
+        peak[at, 0:1, :] = best
+        copies = [
+            (d, send(peak.at[at, one_row], slots.at[d, one_row], to)) for d, to in devices
+        ]
+        for d, copy in copies:
+            copy.wait_recv()
+            best = jnp.maximum(best, slots[d, 0:1, :])
+        return best
+
+    def way(d, n):
+        return min(d, n - d)
+
+    plane = sorted(
+        range(1, 2 * NX * NY), key=lambda d: -way(d // 2 // NY, NX) - way(d // 2 % NY, NY)
+    )
+    line = sorted(range(1, NZ), key=lambda d: -way(d, NZ))
     top = jnp.max(jnp.max(jnp.abs(weight_sum), axis=0), axis=0, keepdims=True)
     best = top[:, 0:128]
     for i in range(1, 4):
         best = jnp.maximum(best, top[:, i * 128 : i * 128 + 128])
-    put_peak(1, best)
-    plane = [
-        send(peak.at[1, one_row], peaks_plane.at[d, one_row], in_plane(d // 2 // NY, d // 2 % NY, d % 2))
-        for d in range(1, 2 * NX * NY)
-    ]
-    for d, copy in enumerate(plane, 1):
-        copy.wait_recv()
-        best = jnp.maximum(best, peaks_plane[d, 0:1, :])
-    put_peak(2, best)
-    way = 1 - 2 * c
-    ring = [
-        send(peak.at[2, one_row], peaks_z.at[k - 1, one_row], along_z(way * k))
-        for k in range(NZ // 2, 0, -1)
-    ]
-    for k, copy in zip(range(NZ // 2, 0, -1), ring):
-        copy.wait_recv()
-        best = jnp.maximum(best, peaks_z[k - 1, 0:1, :])
-    put_peak(3, best)
-    send(peak.at[3, one_row], peaks_end.at[one_row], other_core).wait_recv()
-    amax = jnp.max(jnp.maximum(best, peaks_end[0:1, :]), axis=1, keepdims=True)
+    best = largest(
+        best, 0, peaks_plane, [(d, in_plane(d // 2 // NY, d // 2 % NY, d % 2)) for d in plane]
+    )
+    best = largest(best, 1, peaks_z, [(d, along_z(d)) for d in line])
+    amax = jnp.max(best, axis=1, keepdims=True)
 
     lane = lax.broadcasted_iota(jnp.int32, (1, 16), 1)
     new_history = jnp.where(lane == 0, amax, jnp.roll(hist_ref[...], 1, axis=1))
@@ -357,13 +387,15 @@
 
     @pl.when(even)
     def _():
-        for copy in even_first() + even_then(2) + even_then(6):
-            copy.wait_send()
-
-    @pl.when(jnp.logical_not(even))
+        for p in range(2):
+            for copy in even_first(p) + even_then(p, 2) + even_then(p, 6):
+                copy.wait_send()
+
+    @pl.when(odd)
     def _():
-        for copy in odd_copies():
-            copy.wait_send()
+        for p in range(2):
+            for copy in odd_copies(p):
+                copy.wait_send()
 
     put_ig.wait()
 
@@ -407,15 +439,14 @@
             pltpu.VMEM((2, 2) + part, F32),
             pltpu.VMEM((NB, 2) + part, F32),
             pltpu.VMEM((2 * NX * NY, 8, 128), F32),
-            pltpu.VMEM((NZ // 2, 8, 128), F32),
-            pltpu.VMEM((8, 128), F32),
-            pltpu.VMEM((4, 8, 128), F32),
+            pltpu.VMEM((NZ, 8, 128), F32),
+            pltpu.VMEM((2, 8, 128), F32),
             pltpu.SemaphoreType.DMA((7,)),
             pltpu.SemaphoreType.DMA((N_SENT,)),
             pltpu.SemaphoreType.DMA((N_SENT,)),
-            pltpu.SemaphoreType.DMA((9,)),
-            pltpu.SemaphoreType.DMA((NB,)),
-            pltpu.SemaphoreType.DMA((4,)),
+            pltpu.SemaphoreType.DMA((16,)),
+            pltpu.SemaphoreType.DMA((2 * NB,)),
+            pltpu.SemaphoreType.DMA((8,)),
             pltpu.SemaphoreType.REGULAR((4,)),
         ],
         compiler_params=pltpu.CompilerParams(

time: 97.9 us -> 95.6 us (0.977)
  Pallas kernels: 97.1 us -> 94.7 us
    pallas_call x1, Pallas kernels: 95.4 us -> 93.1 us  [shards(): pl.pallas_call(kernel, out_shape=(jax.ShapeDtypeStruct((192, 512), BF16),...]
where the time goes in v5:
time: 95.6 us; the launch traced here: 95.4 us
  Pallas kernels  94.7 us (99%)
    pallas_call x1, Pallas kernels, shards(): pl.pallas_call(kernel, out_shape=(jax.ShapeDtypeStruct((192, 512), BF16),...  93.1 us

profile of v5, /device:TPU:1, one launch (start us, length us, event | category | flops | bytes accessed | tf_op | source)
XLA Modules:
  0.0 95.4 jit_solution(15903228268689564401)
XLA Ops:
  0.6 93.1 %all_steps.1 = (bf16[192,512]{1,0:T(8,128)(2,1)}, f32[16,512]{1,0:T(8,128)}, f32[1,16]{1,0:T(1,128)}) custom-call(bf16[192,4096]{1,0:T(8,128)(2,1)} %og_hbm.1, bf16[192,512]{1,0:T(8,128)(2,1)} %si_hbm.1, bf16[512,4096]{1,0:T(8,128)(2,1)} %w_hbm.1, f32[1,16]{1,0:T(1,128)} %bitcast.3), custom_call_target="tpu_custom_call" | custom-call | tf_op jit(solution)/shard_map/all_steps/pallas_call | solution.py:413
  93.7 1.6 %write_out.1 = (bf16[192,512]{1,0:T(8,128)(2,1)}, bf16[16,512]{1,0:T(8,128)(2,1)}, f32[1,16]{1,0:T(1,128)}) custom-call(bf16[192,512]{1,0:T(8,128)(2,1)} %get-tuple-element.9.ig_in, f32[16,512]{1,0:T(8,128)} %get-tuple-element.10.wq_in, f32[1,16]{1,0:T(1,128)} %get-tuple-element.11.hist_in), custom_call_target="tpu_custom_call" | custom-call | tf_op jit(solution)/shard_map/write_out/pallas_call | solution.py:457

commit v6 on v5

--- a/solution.py
+++ b/solution.py
@@ -16,9 +16,9 @@
 
 
 def kernel(
-    og_hbm, si_hbm, w_hbm, hist_ref,
+    og_hbm, si_hbm, w_hbm, hist_hbm,
     ig_out, wq_out, hist_out,
-    og, si, w, ig, si_sent, og_sent, si_core, og_core, si_other,
+    hist_ref, og, si, w, ig, si_sent, og_sent, si_core, og_core, si_other,
     terms, pass_one, in_one, pass_two, in_two, ready, relay, relay_far, in_last,
     peaks_plane, peaks_z, peak,
     local_sem, send_sem, recv_sem, last_send, last_recv, relay_sem, hello,
@@ -76,9 +76,11 @@
         for n, k in enumerate(ORDER)
     ]
     get_w = pltpu.make_async_copy(w_hbm, w, local_sem.at[5])
+    get_hist = pltpu.make_async_copy(hist_hbm, hist_ref, local_sem.at[7])
     get_si.start()
     for copy in get_og:
         copy.start()
+    get_hist.start()
 
     used = [0]
     sent = []
@@ -94,7 +96,6 @@
         sent.append(copy)
         return copy
 
-    scale_in = LIMIT / jnp.max(hist_ref[...])
 
     def group(at, i, core):
         return pl.ds(pl.multiple_of(at * 1024 + i * 256 + core * 128, 128), 128)
@@ -114,6 +115,8 @@
         og_copies.append(send(og_sent.at[n], og_core.at[n], other_core))
     get_w.start()
     say(0)
+    get_hist.wait()
+    scale_in = LIMIT / jnp.max(hist_ref[...])
 
     def quantized(grads, inputs):
         term = lax.dot_general(
@@ -329,12 +332,12 @@
             ).wait_recv()
 
     second_start(0)
+    second_start(1)
     second_pass(0)
-    second_start(1)
+    second_pass(1)
     second_end(0)
     hear(3)
     last_start(0)
-    second_pass(1)
     second_end(1)
     last_start(1)
     for p in range(2):
@@ -417,9 +420,10 @@
             jax.ShapeDtypeStruct((16, 512), F32),
             jax.ShapeDtypeStruct((1, 16), F32),
         ),
-        in_specs=[any_space, any_space, any_space, vmem],
+        in_specs=[any_space] * 4,
         out_specs=[any_space, vmem, vmem],
         scratch_shapes=[
+            pltpu.VMEM((1, 16), F32),
             pltpu.VMEM((192, 4096), BF16),
             pltpu.VMEM((192, 512), BF16),
             pltpu.VMEM((512, 4096), BF16),
@@ -441,7 +445,7 @@
             pltpu.VMEM((2 * NX * NY, 8, 128), F32),
             pltpu.VMEM((NZ, 8, 128), F32),
             pltpu.VMEM((2, 8, 128), F32),
-            pltpu.SemaphoreType.DMA((7,)),
+            pltpu.SemaphoreType.DMA((8,)),
             pltpu.SemaphoreType.DMA((N_SENT,)),
             pltpu.SemaphoreType.DMA((N_SENT,)),
             pltpu.SemaphoreType.DMA((16,)),

time: 95.6 us -> 93.5 us (0.978)
  Pallas kernels: 94.7 us -> 92.7 us
    pallas_call x1, Pallas kernels: 93.1 us -> 91.1 us  [shards(): pl.pallas_call(kernel, out_shape=(jax.ShapeDtypeStruct((192, 512), BF16),...]
where the time goes in v6:
time: 93.5 us; the launch traced here: 93.3 us
  Pallas kernels  92.7 us (99%)
    pallas_call x1, Pallas kernels, shards(): pl.pallas_call(kernel, out_shape=(jax.ShapeDtypeStruct((192, 512), BF16),...  91.1 us

profile of v6, /device:TPU:1, one launch (start us, length us, event | category | flops | bytes accessed | tf_op | source)
XLA Modules:
  0.0 93.3 jit_solution(9399867600216654003)
XLA Ops:
  0.6 91.1 %all_steps.1 = (bf16[192,512]{1,0:T(8,128)(2,1)}, f32[16,512]{1,0:T(8,128)}, f32[1,16]{1,0:T(1,128)}) custom-call(bf16[192,4096]{1,0:T(8,128)(2,1)} %og_hbm.1, bf16[192,512]{1,0:T(8,128)(2,1)} %si_hbm.1, bf16[512,4096]{1,0:T(8,128)(2,1)} %w_hbm.1, f32[1,16]{1,0:T(1,128)} %bitcast.3), custom_call_target="tpu_custom_call" | custom-call | tf_op jit(solution)/shard_map/all_steps/pallas_call | solution.py:416
  91.7 1.6 %write_out.1 = (bf16[192,512]{1,0:T(8,128)(2,1)}, bf16[16,512]{1,0:T(8,128)(2,1)}, f32[1,16]{1,0:T(1,128)}) custom-call(bf16[192,512]{1,0:T(8,128)(2,1)} %get-tuple-element.9.ig_in, f32[16,512]{1,0:T(8,128)} %get-tuple-element.10.wq_in, f32[1,16]{1,0:T(1,128)} %get-tuple-element.11.hist_in), custom_call_target="tpu_custom_call" | custom-call | tf_op jit(solution)/shard_map/write_out/pallas_call | solution.py:461

commit v7 on v6

--- a/solution.py
+++ b/solution.py
@@ -12,7 +12,7 @@
 F32, BF16 = jnp.float32, jnp.bfloat16
 ORDER = (2, 1, 3, 0)
 PLACE = {k: n for n, k in enumerate(ORDER)}
-N_SENT = 5 + 12 + 12 + (2 * NX * NY - 1) + (NZ - 1)
+N_SENT = 5 + 12 + 12 + (NX * NY - 1) + (NZ - 1) + 1
 
 
 def kernel(
@@ -311,8 +311,11 @@
 
         @pl.when(odd)
         def _():
-            for copy in odd_copies(p):
+            for copy in odd_copies(p)[:2]:
                 copy.start()
+            if p == 1:
+                for copy in odd_copies(0)[2:] + odd_copies(1)[2:]:
+                    copy.start()
 
     def last_pass(p):
         @pl.when(even)
@@ -366,7 +369,7 @@
         return min(d, n - d)
 
     plane = sorted(
-        range(1, 2 * NX * NY), key=lambda d: -way(d // 2 // NY, NX) - way(d // 2 % NY, NY)
+        range(2, 2 * NX * NY, 2), key=lambda d: -way(d // 2 // NY, NX) - way(d // 2 % NY, NY)
     )
     line = sorted(range(1, NZ), key=lambda d: -way(d, NZ))
     top = jnp.max(jnp.max(jnp.abs(weight_sum), axis=0), axis=0, keepdims=True)
@@ -377,6 +380,7 @@
         best, 0, peaks_plane, [(d, in_plane(d // 2 // NY, d // 2 % NY, d % 2)) for d in plane]
     )
     best = largest(best, 1, peaks_z, [(d, along_z(d)) for d in line])
+    best = largest(best, 2, peaks_plane, [(1, other_core)])
     amax = jnp.max(best, axis=1, keepdims=True)
 
     lane = lax.broadcasted_iota(jnp.int32, (1, 16), 1)
@@ -444,7 +448,7 @@
             pltpu.VMEM((NB, 2) + part, F32),
             pltpu.VMEM((2 * NX * NY, 8, 128), F32),
             pltpu.VMEM((NZ, 8, 128), F32),
-            pltpu.VMEM((2, 8, 128), F32),
+            pltpu.VMEM((3, 8, 128), F32),
             pltpu.SemaphoreType.DMA((8,)),
             pltpu.SemaphoreType.DMA((N_SENT,)),
             pltpu.SemaphoreType.DMA((N_SENT,)),

time: 93.5 us -> 96.7 us (1.034)
  Pallas kernels: 92.7 us -> 95.9 us
    pallas_call x1, Pallas kernels: 91.1 us -> 94.2 us  [shards(): pl.pallas_call(kernel, out_shape=(jax.ShapeDtypeStruct((192, 512), BF16),...]
where the time goes in v7:
time: 96.7 us; the launch traced here: 96.5 us
  Pallas kernels  95.9 us (99%)
    pallas_call x1, Pallas kernels, shards(): pl.pallas_call(kernel, out_shape=(jax.ShapeDtypeStruct((192, 512), BF16),...  94.2 us

profile of v7, /device:TPU:1, one launch (start us, length us, event | category | flops | bytes accessed | tf_op | source)
XLA Modules:
  0.0 96.5 jit_solution(18355926091420593519)
XLA Ops:
  0.6 94.2 %all_steps.1 = (bf16[192,512]{1,0:T(8,128)(2,1)}, f32[16,512]{1,0:T(8,128)}, f32[1,16]{1,0:T(1,128)}) custom-call(bf16[192,4096]{1,0:T(8,128)(2,1)} %og_hbm.1, bf16[192,512]{1,0:T(8,128)(2,1)} %si_hbm.1, bf16[512,4096]{1,0:T(8,128)(2,1)} %w_hbm.1, f32[1,16]{1,0:T(1,128)} %bitcast.3), custom_call_target="tpu_custom_call" | custom-call | tf_op jit(solution)/shard_map/all_steps/pallas_call | solution.py:420
  94.9 1.6 %write_out.1 = (bf16[192,512]{1,0:T(8,128)(2,1)}, bf16[16,512]{1,0:T(8,128)(2,1)}, f32[1,16]{1,0:T(1,128)}) custom-call(bf16[192,512]{1,0:T(8,128)(2,1)} %get-tuple-element.9.ig_in, f32[16,512]{1,0:T(8,128)} %get-tuple-element.10.wq_in, f32[1,16]{1,0:T(1,128)} %get-tuple-element.11.hist_in), custom_call_target="tpu_custom_call" | custom-call | tf_op jit(solution)/shard_map/write_out/pallas_call | solution.py:465
